TPU v7x, 256 devices: a whole 4x4x8 slice. The times are simulated.
256 devices in a mesh: worker: 8 (over x, z_lo), fsdp: 32 (over y, z_hi, core).
Axes of the slice: x: 4, y: 4, z: 8 (z_hi: 4, z_lo: 2; z = z_hi * 2 + z_lo), core: 2. Of those that a mesh axis runs over, the one named last changes fastest.
Arguments:
- tokens: bfloat16 [8, 8192, 7168], P('worker', 'fsdp'), may hold values from -6 to 6
- norm_gain: float32 [8, 7168], P('worker'), may hold values from 0.5 to 1.5
- value_weight: bfloat16 [8, 7168, 512], P('worker', 'fsdp'), may hold values from -0.0625 to 0.0625
- value_cotangent: bfloat16 [8, 8192, 512], P('worker', 'fsdp'), may hold values from -3 to 3
- local_fragments: float32 [8, 16, 524288], P('worker', None, 'fsdp'), may hold values from -6 to 6
- global_fragments: float32 [16, 524288], P(None, 'fsdp'), may hold values from -6 to 6
- outer_velocity: float32 [16, 524288], P(None, 'fsdp'), may hold values from -6 to 6
- fragment_index: int32 [1], replicated, may hold values from 0 to 15
Outputs:
- token_grad: bfloat16 [8, 8192, 7168], P('worker', 'fsdp')
- weight_grad: float32 [8, 7168, 512], P('worker', 'fsdp')
- gain_grad: float32 [8, 7168], P('worker', 'fsdp')
- outer_param: float32 [524288], P('fsdp')
- outer_momentum: float32 [524288], P('fsdp')
All inputs are finite; a program needn't handle non-finite values.
Results may differ from a plain program's by a relative error of at most 0.0031.
Values may be sent and summed in bfloat16 or wider, within the bound.
A program may use at most 128 MiB of HBM per device.

v0:
```python
import jax
import jax.numpy as jnp
from jax import lax
from jax.sharding import PartitionSpec as P

EPSILON = 1e-05
MOMENTUM = 0.9
OUTER_RATE = 0.7


def local(
    tokens,
    norm_gain,
    value_weight,
    value_cotangent,
    local_fragments,
    global_fragments,
    outer_velocity,
    fragment_index,
):
    widened = tokens[0].astype(jnp.float32)
    inverse = lax.rsqrt(jnp.mean(widened * widened, axis=1, keepdims=True) + EPSILON)
    gain_row = norm_gain[0][None, :]
    normed = (widened * inverse * gain_row).astype(jnp.bfloat16)
    upstream = value_cotangent[0]
    d_normed = lax.dot_general(
        upstream,
        lax.all_gather(value_weight, "fsdp", axis=1, tiled=True)[0],
        (((1,), (1,)), ((), ())),
        preferred_element_type=jnp.float32,
    )
    gain_local = jnp.sum(d_normed * widened * inverse, axis=0)[None, :]
    gain_grad = lax.psum_scatter(gain_local, "fsdp", scatter_dimension=1, tiled=True)
    scaled = d_normed * gain_row
    projected = jnp.mean(scaled * widened, axis=1, keepdims=True)
    token_grad = (inverse * (scaled - widened * inverse * inverse * projected)).astype(
        jnp.bfloat16
    )[None]
    weight_local = lax.psum_scatter(
        lax.dot_general(
            normed, upstream, (((0,), (0,)), ((), ())), preferred_element_type=jnp.float32
        ),
        "fsdp",
        scatter_dimension=0,
        tiled=True,
    )
    weight_grad = weight_local[None]
    chosen = fragment_index[0]
    anchor = lax.dynamic_index_in_dim(global_fragments, chosen, 0, keepdims=False)
    replica_part = lax.dynamic_index_in_dim(local_fragments[0], chosen, 0, keepdims=False)
    velocity = lax.dynamic_index_in_dim(outer_velocity, chosen, 0, keepdims=False)
    summed = lax.psum(anchor - replica_part, "worker")
    pseudo_grad = summed / lax.axis_size("worker")
    outer_momentum = MOMENTUM * velocity + pseudo_grad
    outer_param = anchor - OUTER_RATE * (pseudo_grad + MOMENTUM * outer_momentum)
    return (token_grad, weight_grad, gain_grad, outer_param, outer_momentum)


def solution(mesh):
    placed = (
        P("worker", "fsdp", None),
        P("worker", None),
        P("worker", "fsdp", None),
        P("worker", "fsdp", None),
        P("worker", None, "fsdp"),
        P(None, "fsdp"),
        P(None, "fsdp"),
        P(),
    )
    return jax.shard_map(
        local,
        mesh=mesh,
        in_specs=placed,
        out_specs=(
            P("worker", "fsdp", None),
            P("worker", "fsdp", None),
            P("worker", "fsdp"),
            P("fsdp"),
            P("fsdp"),
        ),
        check_vma=False,
    )
```

profile of v0, /device:TPU:6, one launch (start us, length us, event | category | flops | bytes accessed | tf_op | source)
XLA Modules:
  0.0 359.0 jit_solution(5929500786112288955)
XLA Ops:
  8.0 0.0 copy-start
  8.0 0.0 all-gather.2.cloned.1.call-start
  8.1 0.7 all-gather.2.cloned.1.call-update
  8.7 0.0 all-reduce.2.cloned.1.call-start
  9.4 0.0 copy-done
  9.5 0.1 constant_dynamic-slice_fusion.1
  9.5 1.1 constant_dynamic-slice_fusion
  10.6 0.6 sub.10
  11.3 0.0 all-reduce.2.cloned.1.call-update
  11.3 0.0 reduce-scatter.7.cloned.1.call-start
  11.3 2.9 fusion.4
  14.2 74.1 %all-gather.2.cloned.1.call-done = bf16[1,7168,512]{2,1,0:T(8,128)(2,1)} async-done(((bf16[1,224,512]{2,1,0:T(8,128)(2,1)}), bf16[1,7168,512]{2,1,0:T(8,128)(2,1)}) %all-gather.2.cloned.1.call-update) | async-done | bytes 7340048 | tf_op jit(solution)/shard_map/all_gather | solution.py:28
  88.3 9.6 %fusion.12 = (f32[7168]{0:T(1024)S(1)}, f32[256]{0:T(256)S(1)}, f32[256,7168]{1,0:T(8,128)}) fusion(bf16[1,256,7168]{2,1,0:T(8,128)(2,1)} %param.8, f32[256]{0:T(256)S(1)} %add_rsqrt_fusion, f32[7168]{0:T(1024)} %bitcast.64, bf16[1,7168,512]{2,1,0:T(8,128)(2,1)} %all-gather.2.cloned.1.call-done, bf16[1,256,512]{2,1,0:T(8,128)(2,1)} %param.11), kind=kOutput, calls=%fused_computation.14 | convolution fusion | flops 1891885824 | bytes 18671616 | tf_op jit(solution)/shard_map/dot_general | solution.py:26
  97.9 0.0 copy-start.1
  97.9 0.0 copy-start.2
  97.9 2.5 copy.13
  100.4 0.0 reduce-scatter.7.cloned.1.call-update
  100.4 0.0 reduce-scatter.5.cloned.1.call-start
  100.5 0.0 copy-done.1
  100.5 0.0 copy-done.2
  100.5 9.5 %fusion.18 = f32[7168,512]{1,0:T(8,128)} fusion(bf16[1,256,7168]{2,1,0:T(8,128)(2,1)} %param.8, f32[7168]{0:T(1024)S(1)} %bitcast.65, f32[256]{0:T(256)S(1)} %add_rsqrt_fusion, bf16[1,256,512]{2,1,0:T(8,128)(2,1)S(1)} %copy-done.1), kind=kOutput, calls=%fused_computation.20 | convolution fusion | flops 1886388224 | bytes 18641920 | tf_op jit(solution)/shard_map/dot_general | solution.py:40
  110.0 0.0 reduce-scatter.5.cloned.1.call-update
  110.0 1.1 dynamic-slice_multiply_fusion
  111.1 0.0 all-reduce.2.cloned.1.call-done
  111.2 1.5 multiply_subtract_fusion
  112.7 6.7 %fusion.20 = bf16[1,256,7168]{2,1,0:T(8,128)(2,1)} fusion(bf16[1,256,7168]{2,1,0:T(8,128)(2,1)} %param.8, f32[256,7168]{1,0:T(8,128)} %get-tuple-element.9, f32[256]{0:T(256)S(1)} %broadcast_multiply_fusion, f32[7168]{0:T(1024)S(1)} %bitcast.66, f32[256]{0:T(256)S(1)} %add_rsqrt_fusion), kind=kLoop, calls=%fused_computation.21 | loop fusion | flops 14680064 | bytes 14710784 | tf_op jit(solution)/shard_map/broadcast_in_dim | solution.py:36
  119.4 76.6 %reduce-scatter.7.cloned.1.call-done = f32[224,1]{1,0:T(8,128)} async-done(((f32[7168,1]{1,0:T(8,128)}), f32[224,1]{1,0:T(8,128)}) %reduce-scatter.7.cloned.1.call-update) | async-done | bytes 912
  196.0 1.5 copy.14
  197.5 154.4 %reduce-scatter.5.cloned.1.call-done = f32[224,512]{1,0:T(8,128)} async-done(((f32[7168,512]{1,0:T(8,128)}), f32[224,512]{1,0:T(8,128)}) %reduce-scatter.5.cloned.1.call-update) | async-done | bytes 458768 | tf_op jit(solution)/shard_map/reduce_scatter | solution.py:39
  (2 shorter events, 0.0 us)
Async XLA Ops:
  8.0 1.5 copy-start
  8.0 80.3 %all-gather.2.cloned.1.call-start = ((), (), s32[]{:S(2)}) async-start(), calls=%async_computation.2 | async-start | bytes 7569408 | tf_op jit(solution)/shard_map/all_gather | solution.py:28
  8.7 102.4 %all-reduce.2.cloned.1.call-start = ((), (), s32[]{:S(2)}) async-start(), calls=%async_computation.4 | async-start | bytes 131072 | tf_op jit(solution)/shard_map/psum | solution.py:52
  11.3 184.7 %reduce-scatter.7.cloned.1.call-start = ((), (), s32[]{:S(2)}) async-start(), calls=%async_computation.5 | async-start | bytes 3784704
  97.9 2.6 copy-start.1
  97.9 2.6 copy-start.2
  100.4 251.5 %reduce-scatter.5.cloned.1.call-start = ((), (), s32[]{:S(2)}) async-start(), calls=%async_computation.3 | async-start | bytes 15138816 | tf_op jit(solution)/shard_map/reduce_scatter | solution.py:39
Sparse Core Ops, SparseCore 0:
  11.4 76.8 all-gather.1
  100.5 95.3 reduce-scatter.6
  201.3 150.5 reduce-scatter.4
Sparse Core Ops, SparseCore 1:
  12.4 88.5 all-reduce.1
where the time goes:
time: 359 us
  waiting for transfers between devices  306 us (85%)
  matrix products  19 us (5%)
  between operations  15.9 us (4%)
  other arithmetic  12.8 us (4%)
  local copies, waits for them, and re-layouts  5.2 us (1%)
    reduce_scatter x1, waiting for transfers between devices, local(): lax.psum_scatter(lax.dot_general(normed, upstream, (((0,), (0,)), ((), ()...  154 us
    unnamed x5, waiting for transfers between devices  77.3 us
    all_gather x1, waiting for transfers between devices, local(): lax.all_gather(value_weight, 'fsdp', axis=1, tiled=True)[0]  74.1 us
    dot_general x1, matrix products, local(): lax.dot_general(upstream, lax.all_gather(value_weight, 'fsdp', axis=1, ti...  9.56 us
    dot_general x1, matrix products, local(): lax.dot_general(normed, upstream, (((0,), (0,)), ((), ())), preferred_ele...  9.46 us
  transfers between devices with their start and end apart: 4, of which 3 were waited for; matrix products, arithmetic and copies ran while one was open for 10% of the time, Pallas kernels for 0%

commit v1 on v0

v1 whole, which is shorter than its diff:
```python
import functools

import jax
import jax.numpy as jnp
from jax import lax
from jax.experimental import pallas as pl
from jax.experimental.pallas import tpu as pltpu
from jax.sharding import PartitionSpec as P

EPSILON = 1e-05
MOMENTUM = 0.9
OUTER_RATE = 0.7
MESH = pl.DeviceIdType.MESH
RING = 4
NT = (((1,), (1,)), ((), ()))
SEMS = 120
GATHER_PARTS = ((0, 224, "z"),)
SCATTER_PARTS = ((0, 128, "y"), (128, 224, "z"))


def kernel(
    tokens,
    gain,
    weight,
    cotangent,
    difference,
    anchor,
    velocity,
    token_out,
    weight_out,
    gain_out,
    param_out,
    momentum_out,
    tok,
    turned,
    turned_other,
    cot,
    full,
    part,
    scaled,
    inverse,
    projected,
    x_in,
    z_out,
    z_in,
    *rest,
):
    buffers, (send_sem, recv_sem, local_sem) = rest[:-3], rest[-3:]
    rows, features = tok.shape
    block = weight.shape[0]
    values = weight.shape[1]

    worker = lax.axis_index("worker")
    place = lax.axis_index("fsdp")
    core = lax.rem(place, 2)
    z = lax.rem(place // 2, RING)
    y = place // (2 * RING)
    x, low = worker // 2, lax.rem(worker, 2)

    chip = {
        (dy, dz): lax.rem(y + dy, RING) * RING + lax.rem(z + dz, RING)
        for dy in range(RING)
        for dz in range(RING)
    }

    def device(dy, dz):
        return {"fsdp": 2 * chip[dy, dz] + core}

    partner = {"fsdp": place + 1 - 2 * core}
    beside_x = [{"worker": lax.rem(x + d, RING) * 2 + low} for d in (1, 2, 3)]
    beside_low = {"worker": x * 2 + 1 - low}

    numbers = {}

    def copy(key, src, dst, target):
        index = numbers.setdefault(key, len(numbers))
        return pltpu.make_async_remote_copy(
            src_ref=src,
            dst_ref=dst,
            send_sem=send_sem.at[index],
            recv_sem=recv_sem.at[index],
            device_id=target,
            device_id_type=MESH,
        )

    sent = []

    def send(key, src, dst, target):
        c = copy(key, src, dst, target)
        c.start()
        sent.append(c)

    def arrive(key, dst, target):
        copy(key, dst, dst, target).wait_recv()

    token_copies = []
    half_rows = rows // 2
    for i in range(2):
        span = pl.ds(i * half_rows, half_rows)
        token_copies.append(
            pltpu.make_async_copy(tokens.at[span], tok.at[span], local_sem.at[i])
        )
    cot_copy = pltpu.make_async_copy(cotangent, cot.at[0], local_sem.at[2])
    own = pl.ds(pl.multiple_of(place * block, 16), block)
    own_copy = pltpu.make_async_copy(weight, full.at[own], local_sem.at[3])
    for c in token_copies:
        c.start()
    cot_copy.start()
    own_copy.start()

    greeted = [partner, *beside_x, beside_low]
    greeted += [device(1, 0), device(3, 0), device(0, 1), device(0, 3)]
    barrier = pltpu.get_barrier_semaphore()
    for target in greeted:
        pl.semaphore_signal(barrier, inc=1, device_id=target, device_id_type=MESH)
    pl.semaphore_wait(barrier, len(greeted))

    events = []

    def at(time, fn, *args):
        events.append((time, len(events), functools.partial(fn, *args)))

    def slot(dy, dz, which, lo, hi):
        start = (2 * chip[dy, dz] + which) * block + lo
        return full.at[pl.ds(pl.multiple_of(start, 16), hi - lo)]

    def gather(number, lo, hi, first, times):
        mid = (lo + hi) // 2
        halves = {1: (lo, mid), 3: (mid, hi)}

        def at_offset(a, b):
            return (b, a) if first == "z" else (a, b)

        def to_first(s):
            return device(*at_offset(s, 0))

        def to_second(s):
            return device(*at_offset(0, s))

        def held(a, b, which=core, span=(lo, hi)):
            return slot(*at_offset(a, b), which, *span)

        def exchange(a, b, src=None):
            here = held(a, b)
            send((number, "x", a, b), here if src is None else src, here, partner)

        def spread(a, src=None):
            here = held(a, 0)
            for s in (1, 3):
                send((number, "b", a, s), here if src is None else src, here, to_second(s))

        def begin():
            src = weight.at[pl.ds(lo, hi - lo)]
            for s in (1, 3):
                send((number, "a", s), src, held(0, 0), to_first(s))
            spread(0, src)
            exchange(0, 0, src)

        def first_near():
            for s in (1, 3):
                arrive((number, "a", s), held(4 - s, 0), to_first(s))
                piece = held(4 - s, 0, core, halves[s])
                send((number, "af", s), piece, piece, to_first(s))
            for s in (1, 3):
                spread(4 - s)
            for s in (1, 3):
                exchange(4 - s, 0)

        def first_far():
            for s in (1, 3):
                arrive((number, "af", s), held(2, 0, core, halves[s]), to_first(s))
            spread(2)
            exchange(2, 0)

        def second_near(a):
            for s in (1, 3):
                arrive((number, "b", a, s), held(a, 4 - s), to_second(s))
                piece = held(a, 4 - s, core, halves[s])
                send((number, "bf", a, s), piece, piece, to_second(s))
            for s in (1, 3):
                exchange(a, 4 - s)

        def second_far(a):
            for s in (1, 3):
                arrive((number, "bf", a, s), held(a, 2, core, halves[s]), to_second(s))
            exchange(a, 2)

        def settled(dy):
            for dz in range(RING):
                a, b = (dz, dy) if first == "z" else (dy, dz)
                arrive((number, "x", a, b), held(a, b, 1 - core), partner)

        at(times["begin"], begin)
        at(times["first_near"], first_near)
        at(times["first_far"], first_far)
        for a in (0, 3, 1, 2):
            at(times["near"][a], second_near, a)
            at(times["far"][a], second_far, a)
        return settled

    span = features // RING

    def project(dy):
        start = pl.multiple_of(lax.rem(y + dy, RING) * span, 128)

        @pl.loop(0, span // 256)
        def _(i):
            here = pl.ds(pl.multiple_of(start + i * 256, 128), 256)
            d = lax.dot_general(
                cot[0], full[here, :], NT, preferred_element_type=jnp.float32
            )
            s = d * gain[:, here]
            scaled[:, here] = s
            both = s * tok[:, here].astype(jnp.float32)
            projected[...] += both[:, :128] + both[:, 128:]

    def finish_tokens():
        step = 32

        @pl.loop(0, rows // step)
        def _(i):
            here = pl.ds(pl.multiple_of(i * step, step), step)
            inv = inverse[here, :]
            mean = jnp.sum(projected[here, :], axis=1, keepdims=True) / features
            back = inv * inv * mean

            @pl.loop(0, features // 1024)
            def _(j):
                cols = pl.ds(pl.multiple_of(j * 1024, 128), 1024)
                wide = tok[here, cols].astype(jnp.float32)
                tok[here, cols] = (inv * (scaled[here, cols] - wide * back)).astype(
                    jnp.bfloat16
                )

            pltpu.make_async_copy(tok.at[here], token_out.at[here], local_sem.at[4]).start()

        pltpu.make_async_copy(tok, token_out, local_sem.at[4]).wait()

    def normalize():
        for i in range(2):
            token_copies[i].wait()
            here = pl.ds(i * half_rows, half_rows)

            def square(j, total):
                wide = tok[here, pl.ds(pl.multiple_of(j * 256, 128), 256)].astype(
                    jnp.float32
                )
                wide = wide * wide
                return total + wide[:, :128] + wide[:, 128:]

            total = lax.fori_loop(
                0, features // 256, square, jnp.zeros((half_rows, 128), jnp.float32)
            )
            inv = lax.rsqrt(jnp.sum(total, axis=1, keepdims=True) / features + EPSILON)
            inverse[here, :] = inv

            @pl.loop(0, features // (4 * block))
            def _(j):
                cols = pl.ds(pl.multiple_of(j * 4 * block, 128), 4 * block)
                normed = (
                    tok[here, cols].astype(jnp.float32) * inv * gain[:, cols]
                ).astype(jnp.bfloat16)
                flipped = normed.T
                for b in range(4):
                    turned[2 * j + b // 2, b % 2, :, here] = flipped[
                        b * block : (b + 1) * block
                    ]

        for q in range(RING):
            here = pl.ds(q * RING, RING)
            send(("t", q), turned.at[here, 1 - core], turned_other.at[here], partner)

    def own_products():
        cot_copy.wait()

        @pl.loop(0, RING * RING)
        def _(k):
            part[k] = jnp.dot(
                turned[k, core], cot[0], preferred_element_type=jnp.float32
            )

    def other_products():
        arrive("cot", cot.at[1], partner)
        for q in range(RING):
            arrive(("t", q), turned_other.at[pl.ds(q * RING, RING)], partner)

        @pl.loop(0, RING * RING)
        def _(k):
            part[k] += jnp.dot(
                turned_other[k], cot[1], preferred_element_type=jnp.float32
            )

    def scatter(number, lo, hi, first, refs, times):
        far_out, far_in, near_out, near_in, far2_out, far2_in, near2_out, near2_in, total = (
            refs
        )
        size = hi - lo
        halves = {1: pl.ds(0, size // 2), 3: pl.ds(size // 2, size // 2)}
        other = {1: halves[3], 3: halves[1]}
        index = {1: 0, 3: 1}
        start = {1: lo, 3: lo + size // 2}

        def at_offset(a, b):
            return (b, a) if first == "z" else (a, b)

        def to_first(s):
            return device(*at_offset(s, 0))

        def to_second(s):
            return device(*at_offset(0, s))

        def mine(a, b, s=None):
            span = pl.ds(lo, size) if s is None else pl.ds(start[s], size // 2)
            return part[chip[at_offset(a, b)], span, :]

        def far(b):
            for s in (1, 3):
                far_out[b, halves[s], :] = mine(2, b, s).astype(jnp.bfloat16)
                send(
                    (number, "f", b, s),
                    far_out.at[b, halves[s]],
                    far_in.at[b, halves[s]],
                    to_first(s),
                )

        def near(b):
            for s in (1, 3):
                i = index[s]
                near_out[i, b, other[s], :] = mine(s, b, 4 - s).astype(jnp.bfloat16)
                arrive((number, "f", b, s), far_in.at[b, halves[s]], to_first(s))
                near_out[i, b, halves[s], :] = (
                    mine(s, b, s) + far_in[b, halves[s], :].astype(jnp.float32)
                ).astype(jnp.bfloat16)
                send((number, "n", b, s), near_out.at[i, b], near_in.at[i, b], to_first(s))

        def gathered(b):
            for s in (1, 3):
                arrive((number, "n", b, s), near_in.at[index[s], b], to_first(s))
            total[b] = (
                mine(0, b)
                + near_in[0, b].astype(jnp.float32)
                + near_in[1, b].astype(jnp.float32)
            )

        def far2():
            for s in (1, 3):
                far2_out[halves[s], :] = total[2, halves[s], :].astype(jnp.bfloat16)
                send(
                    (number, "f2", s),
                    far2_out.at[halves[s]],
                    far2_in.at[halves[s]],
                    to_second(s),
                )

        def near2(s):
            i = index[s]
            near2_out[i, other[s], :] = total[s, other[s], :].astype(jnp.bfloat16)
            arrive((number, "f2", s), far2_in.at[halves[s]], to_second(s))
            near2_out[i, halves[s], :] = (
                total[s, halves[s], :] + far2_in[halves[s], :].astype(jnp.float32)
            ).astype(jnp.bfloat16)
            send((number, "n2", s), near2_out.at[i], near2_in.at[i], to_second(s))

        def final():
            for s in (1, 3):
                arrive((number, "n2", s), near2_in.at[index[s]], to_second(s))
            weight_out[pl.ds(lo, size), :] = (
                total[0]
                + near2_in[0].astype(jnp.float32)
                + near2_in[1].astype(jnp.float32)
            )

        order = (2, 1, 3, 0)
        for j, b in enumerate(order):
            at(times["far"][j], far, b)
            at(times["near"][j], near, b)
            at(times["sum"][j], gathered, b)
        at(times["sum"][0] + 0.01, far2)
        at(times["sum"][1] + 0.01, near2, 1)
        at(times["sum"][2] + 0.01, near2, 3)
        at(times["final"], final)

    def gain_gradient():
        product = weight_out[...] * full[own, :].astype(jnp.float32)
        ones = jnp.ones((8, values), jnp.float32)
        sums = lax.dot_general(
            ones,
            product,
            NT,
            preferred_element_type=jnp.float32,
            precision=lax.Precision.HIGHEST,
        )[0:1]
        group = gain[:, pl.ds(pl.multiple_of((place // 4) * 4 * block, 128), 4 * block)]
        which = lax.rem(place, 4)
        scale = group[:, :block]
        for i in range(1, 4):
            scale = jnp.where(which == i, group[:, i * block : (i + 1) * block], scale)
        gain_out[...] = sums / scale

    def outer_begin():
        x_in[x] = difference[...]
        for i, target in enumerate(beside_x):
            send(("ox", i), difference, x_in.at[x], target)

    def outer_middle():
        for i, target in enumerate(beside_x):
            arrive(("ox", i), x_in.at[lax.rem(x + RING - 1 - i, RING)], target)
        z_out[...] = x_in[0] + x_in[1] + x_in[2] + x_in[3]
        send("oz", z_out, z_in, beside_low)

    def outer_end():
        arrive("oz", z_in, beside_low)
        pseudo = (z_out[...] + z_in[...]) / 8
        momentum = MOMENTUM * velocity[...] + pseudo
        momentum_out[...] = momentum
        param_out[...] = anchor[...] - OUTER_RATE * (pseudo + MOMENTUM * momentum)

    def send_cotangent():
        send("cot", cotangent, cot.at[1], partner)

    def clear():
        projected[...] = jnp.zeros_like(projected)

    settled = []
    settled.append(
        gather(
            "g0",
            *GATHER_PARTS[0],
            dict(
                begin=0,
                first_near=9.5,
                first_far=14,
                near={0: 6, 3: 16.5, 1: 16.6, 2: 27},
                far={0: 9, 3: 23.5, 1: 23.6, 2: 32},
            ),
        )
    )
    at(0.5, send_cotangent)
    at(0.6, outer_begin)
    at(1, clear)
    at(2, normalize)
    at(7, own_products)
    at(9.4, other_products)
    scatter(
        "s0",
        *SCATTER_PARTS[0],
        buffers[:9],
        dict(far=(10, 10.1, 15, 22), near=(13, 17, 25, 31), sum=(21, 28, 34, 38), final=46),
    )
    scatter(
        "s1",
        *SCATTER_PARTS[1],
        buffers[9:],
        dict(far=(10.2, 10.3, 17.1, 24), near=(14.1, 20, 26, 31.2), sum=(22, 29, 35, 39), final=45),
    )
    at(20, outer_middle)
    at(30, outer_end)

    def settle_and_project(dy):
        for fn in settled:
            fn(dy)
        project(dy)

    at(19, lambda: own_copy.wait())
    at(19.1, settle_and_project, 0)
    at(40, settle_and_project, 3)
    at(40.1, settle_and_project, 1)
    at(40.2, settle_and_project, 2)
    at(40.3, finish_tokens)

    at(47, gain_gradient)
    for _, _, fn in sorted(events, key=lambda e: e[:2]):
        fn()
    for c in sent:
        c.wait_send()


def local(
    tokens,
    norm_gain,
    value_weight,
    value_cotangent,
    local_fragments,
    global_fragments,
    outer_velocity,
    fragment_index,
):
    chosen = fragment_index[0]
    anchor = lax.dynamic_index_in_dim(global_fragments, chosen, 0, keepdims=False)
    replica_part = lax.dynamic_index_in_dim(local_fragments[0], chosen, 0, keepdims=False)
    velocity = lax.dynamic_index_in_dim(outer_velocity, chosen, 0, keepdims=False)
    square = (-1, 128)
    anchor, velocity = anchor.reshape(square), velocity.reshape(square)
    difference = anchor - replica_part.reshape(square)
    lines = anchor.shape[0]

    _, rows, features = tokens.shape
    _, block, values = value_weight.shape
    blocks = RING * RING
    vmem = pltpu.VMEM
    bf16, f32 = jnp.bfloat16, jnp.float32
    scratch = [
        vmem((rows, features), bf16),
        vmem((blocks, 2, block, rows), bf16),
        vmem((blocks, block, rows), bf16),
        vmem((2, rows, values), bf16),
        vmem((features, values), bf16),
        vmem((blocks, block, values), f32),
        vmem((rows, features), f32),
        vmem((rows, 1), f32),
        vmem((rows, 128), f32),
        vmem((RING, lines, 128), f32),
        vmem((lines, 128), f32),
        vmem((lines, 128), f32),
    ]
    for lo, hi, _ in SCATTER_PARTS:
        size = hi - lo
        scratch += [
            vmem((RING, size, values), bf16),
            vmem((RING, size, values), bf16),
            vmem((2, RING, size, values), bf16),
            vmem((2, RING, size, values), bf16),
            vmem((size, values), bf16),
            vmem((size, values), bf16),
            vmem((2, size, values), bf16),
            vmem((2, size, values), bf16),
            vmem((RING, size, values), f32),
        ]
    scratch += [
        pltpu.SemaphoreType.DMA((SEMS,)),
        pltpu.SemaphoreType.DMA((SEMS,)),
        pltpu.SemaphoreType.DMA((5,)),
    ]
    in_vmem = pl.BlockSpec(memory_space=pltpu.VMEM)
    in_hbm = pl.BlockSpec(memory_space=pl.ANY)
    token_grad, weight_grad, gain_grad, param, momentum = pl.pallas_call(
        kernel,
        out_shape=(
            jax.ShapeDtypeStruct((rows, features), bf16),
            jax.ShapeDtypeStruct((block, values), f32),
            jax.ShapeDtypeStruct((1, block), f32),
            jax.ShapeDtypeStruct((lines, 128), f32),
            jax.ShapeDtypeStruct((lines, 128), f32),
        ),
        in_specs=[in_hbm, in_vmem, in_hbm, in_hbm, in_vmem, in_vmem, in_vmem],
        out_specs=(in_hbm, in_vmem, in_vmem, in_vmem, in_vmem),
        scratch_shapes=scratch,
        compiler_params=pltpu.CompilerParams(
            collective_id=0, has_side_effects=True, vmem_limit_bytes=58 * 2**20
        ),
        cost_estimate=pl.CostEstimate(
            flops=4 * rows * features * values, bytes_accessed=2**24, transcendentals=0
        ),
    )(
        tokens[0],
        norm_gain,
        value_weight[0],
        value_cotangent[0],
        difference,
        anchor,
        velocity,
    )
    return (
        token_grad[None],
        weight_grad[None],
        gain_grad,
        param.reshape(-1),
        momentum.reshape(-1),
    )


def solution(mesh):
    placed = (
        P("worker", "fsdp", None),
        P("worker", None),
        P("worker", "fsdp", None),
        P("worker", "fsdp", None),
        P("worker", None, "fsdp"),
        P(None, "fsdp"),
        P(None, "fsdp"),
        P(),
    )
    return jax.shard_map(
        local,
        mesh=mesh,
        in_specs=placed,
        out_specs=(
            P("worker", "fsdp", None),
            P("worker", "fsdp", None),
            P("worker", "fsdp"),
            P("fsdp"),
            P("fsdp"),
        ),
        check_vma=False,
    )
```

time: 359 us -> 96.7 us (0.27)
  waiting for transfers between devices: 306 us -> 0 us
  Pallas kernels: 0 us -> 84.4 us
  matrix products: 19 us -> 0 us
  between operations: 15.9 us -> 1.43 us
  other arithmetic: 12.8 us -> 0.65 us
  local copies, waits for them, and re-layouts: 5.2 us -> 9.26 us
    reduce_scatter x1 -> x0, waiting for transfers between devices: 154 us -> none  [local(): lax.psum_scatter(lax.dot_general(normed, upstream, (((0,), (0,)), ((), ()...]
    pallas_call x0 -> x1, Pallas kernels: none -> 84.4 us  [local(): pl.pallas_call(kernel, out_shape=(jax.ShapeDtypeStruct((rows, features),...]
    unnamed x5 -> x0, waiting for transfers between devices: 77.3 us -> none
    all_gather x1 -> x0, waiting for transfers between devices: 74.1 us -> none  [local(): lax.all_gather(value_weight, 'fsdp', axis=1, tiled=True)[0]]
    dot_general x2 -> x0, matrix products: 19 us -> none  [the longest x1 9.56 us: local(): lax.dot_general(upstream, lax.all_gather(value_weight, 'fsdp', axis=1, ti...]
    broadcast_in_dim x1 -> x0, other arithmetic: 6.69 us -> none  [local(): (inverse * (scaled - widened * inverse * inverse * projected)).astype(jnp...]
    unnamed x8 -> x17, local copies, waits for them, and re-layouts: 4.05 us -> 7.28 us
  transfers between devices with their start and end apart: 4 -> 0, of which waited for: 3 -> 0; matrix products, arithmetic and copies ran while one was open for 10% -> 0% of each run, Pallas kernels for 0% -> 0%
where the time goes in v1:
time: 96.7 us; the launch traced here: 95.7 us
  Pallas kernels  84.4 us (87%)
  local copies, waits for them, and re-layouts  9.26 us (10%)
  between operations  1.43 us (1%)
    pallas_call x1, Pallas kernels, local(): pl.pallas_call(kernel, out_shape=(jax.ShapeDtypeStruct((rows, features),...  84.4 us
    unnamed x17, local copies, waits for them, and re-layouts  7.28 us

profile of v1, /device:TPU:6, one launch (start us, length us, event | category | flops | bytes accessed | tf_op | source)
XLA Modules:
  0.0 95.7 jit_solution(193573701752061473)
XLA Ops:
  0.6 0.0 copy-start
  1.4 0.5 copy-done
  1.9 1.9 %constant_dynamic-slice_fusion = (f32[1,16384]{1,0:T(1,128)}, f32[1,16384]{1,0:T(1,128)S(1)}) fusion(f32[16,16384]{1,0:T(8,128)} %param.14, s32[]{:T(128)S(6)} %select_n.6, f32[16,16384]{1,0:T(8,128)} %param.13), kind=kLoop, calls=%fused_computation | loop fusion | bytes 262148 | tf_op jit(solution)/shard_map/jit(dynamic_index_in_dim)/dynamic_slice | solution.py:491
  3.9 0.0 copy-start.2
  3.9 0.6 sub.3.difference
  4.5 0.0 copy-done.2
  4.5 84.4 %shard_map.119 = (bf16[256,7168]{1,0:T(8,128)(2,1)}, f32[224,512]{1,0:T(8,128)}, f32[1,224]{1,0:T(1,128)}, f32[128,128]{1,0:T(8,128)}, f32[128,128]{1,0:T(8,128)}) custom-call(bf16[256,7168]{1,0:T(8,128)(2,1)} %bitcast.22, f32[1,7168]{1,0:T(1,128)} %gain.1, bf16[224,512]{1,0:T(8,128)(2,1)} %bitcast.24, bf16[256,512]{1,0:T(8,128)(2,1)} %bitcast.23, ...), custom_call_target="tpu_custom_call" | custom-call | flops 3758096384 | bytes 16777216 | tf_op jit(solution)/shard_map/pallas_call | solution.py:536
  88.9 0.0 copy-start.1
  88.9 0.0 copy-start.5
  88.9 0.0 copy-start.4
  88.9 0.0 copy-start.3
  88.9 4.2 %copy.19 = bf16[1,256,7168]{2,1,0:T(8,128)(2,1)} copy(bf16[1,256,7168]{2,1,0:T(8,128)(2,1)} %bitcast.14) | data formatting | bytes 7340032
  93.1 0.0 copy-done.1
  93.1 0.8 copy.20
  93.9 0.0 copy-done.5
  93.9 0.6 copy.21
  94.4 0.0 copy-done.4
  94.4 0.6 copy.22
  95.1 0.0 copy-done.3
  95.1 0.6 copy.23
  (1 shorter events, 0.0 us)
Async XLA Ops:
  0.6 1.2 %copy-start = (f32[1,16,16384]{2,1,0:T(8,128)S(1)}, f32[1,16,16384]{2,1,0:T(8,128)}, u32[]{:S(2)}) copy-start(f32[1,16,16384]{2,1,0:T(8,128)} %param.12) | copy-start | bytes 3145732
  3.9 0.7 copy-start.2
  88.9 4.2 %copy-start.1 = (f32[224,512]{1,0:T(8,128)S(1)}, f32[224,512]{1,0:T(8,128)}, u32[]{:S(2)}) copy-start(f32[224,512]{1,0:T(8,128)} %get-tuple-element.11) | copy-start | bytes 1376260
  88.9 5.0 %copy-start.5 = (f32[1,224]{1,0:T(1,128)S(1)}, f32[1,224]{1,0:T(1,128)}, u32[]{:S(2)}) copy-start(f32[1,224]{1,0:T(1,128)} %get-tuple-element.24) | copy-start | bytes 2692
  88.9 5.5 %copy-start.4 = (f32[128,128]{1,0:T(8,128)S(1)}, f32[128,128]{1,0:T(8,128)}, u32[]{:S(2)}) copy-start(f32[128,128]{1,0:T(8,128)} %get-tuple-element.13) | copy-start | bytes 196612
  88.9 6.2 %copy-start.3 = (f32[128,128]{1,0:T(8,128)S(1)}, f32[128,128]{1,0:T(8,128)}, u32[]{:S(2)}) copy-start(f32[128,128]{1,0:T(8,128)} %get-tuple-element.14) | copy-start | bytes 196612

commit v2 on v0

v2 whole, which is shorter than its diff:
```python
import functools
import types

import jax
import jax.numpy as jnp
from jax import lax
from jax.experimental import pallas as pl
from jax.experimental.pallas import tpu as pltpu
from jax.sharding import PartitionSpec as P

EPSILON = 1e-05
MOMENTUM = 0.9
OUTER_RATE = 0.7
MESH = pl.DeviceIdType.MESH
RING = 4
NT = (((1,), (1,)), ((), ()))
GATHER_PARTS = ((0, 64, "z"), (64, 128, "z"), (128, 224, "z"))
SCATTER_PARTS = ((0, 64, "y"), (64, 128, "y"), (128, 224, "z"))
WIDTH = 512
ORDER = (
    0, 32, 16, 48, 49, 4, 50, 52, 54, 5, 1, 2, 20, 21, 51, 106, 86, 66, 56, 6, 58, 33, 8, 34,
    126, 11, 10, 22, 18, 17, 129, 36, 53, 3, 67, 110, 55, 114, 68, 127, 57, 59, 118, 90, 42, 39,
    35, 87, 12, 107, 19, 26, 27, 70, 108, 94, 24, 74, 43, 37, 13, 14, 88, 40, 23, 69, 82, 7, 60,
    62, 64, 128, 46, 61, 112, 63, 115, 30, 45, 65, 72, 111, 132, 116, 76, 29, 28, 44, 71, 109,
    122, 38, 95, 75, 96, 15, 133, 120, 25, 89, 102, 9, 41, 92, 119, 47, 91, 134, 31, 73, 83,
    135, 98, 136, 113, 123, 78, 137, 77, 84, 97, 117, 124, 93, 103, 99, 100, 104, 130, 80, 121,
    79, 131, 138, 140, 101, 125, 81, 85, 105, 139,
)
OPPOSITE = {1: 3, 3: 1, 2: 2}
CHUNKS = ((2, 1), (1, 1), (3, 1), (2, 0), (0, 1), (1, 0), (3, 0), (0, 0))


class Event:
    def __init__(self, name, body, cost, rank, needs=(), after=(), sends=()):
        self.name, self.body, self.cost, self.rank = name, body, cost, rank
        self.needs, self.after, self.sends = list(needs), list(after), list(sends)


def build(env, rows, features, block):
    events = []

    def add(name, *args, **kw):
        events.append(Event(name, *args, **kw))

    def nothing():
        pass

    chunk_of = {c: i for i, c in enumerate(CHUNKS)}

    def product(dy, dz):
        sides = {0: (0,), 2: (1,), 1: (0, 1), 3: (0, 1)}[dz]
        return [("product", chunk_of[dy, s]) for s in sides]

    def gather(number, lo, hi, first):
        mid = (lo + hi) // 2
        halves = {1: (lo, mid), 3: (mid, hi)}
        second = "y" if first == "z" else "z"
        full_size, half_size = (hi - lo) * WIDTH * 2, (hi - lo) * WIDTH

        def offset(a, b):
            return (b, a) if first == "z" else (a, b)

        def target(axis, s):
            return env.device(0, s) if axis == "z" else env.device(s, 0)

        def held(a, b, span=(lo, hi), other=False):
            which = 1 - env.core if other else env.core
            return env.slot(*offset(a, b), which, *span)

        def whole(key, axis, s, a, b, own=False):
            def refs():
                here = held(a, b)
                src = env.weight.at[pl.ds(lo, hi - lo)] if own else here
                return src, here, target(axis, s)

            return (number, *key), axis + str(s), full_size, refs

        def half(key, axis, s, a, b):
            def refs():
                here = held(a, b, halves[s])
                return here, here, target(axis, s)

            return (number, *key), axis + str(s), half_size, refs

        def exchange(a, b, own=False):
            def refs():
                here = held(a, b)
                src = env.weight.at[pl.ds(lo, hi - lo)] if own else here
                return src, here, env.partner

            return (number, "x", a, b), "c", full_size, refs

        def need(key, axis, s, a, b, part=False):
            def refs():
                return held(a, b, halves[s] if part else (lo, hi)), target(axis, s)

            return (number, *key), refs

        def spread(a, own=False):
            return [whole(("b", a, s), second, s, a, 0, own) for s in (1, 3)]

        add(
            (number, "begin"),
            nothing,
            0.1,
            0,
            sends=[whole(("a", s), first, s, 0, 0, True) for s in (1, 3)]
            + spread(0, True)
            + [exchange(0, 0, True)],
        )
        for s in (1, 3):
            a = OPPOSITE[s]
            add(
                (number, "first", s),
                nothing,
                0.1,
                1,
                needs=[need(("a", s), first, s, a, 0)],
                sends=[half(("af", s), first, s, a, 0), *spread(a), exchange(a, 0)],
            )
        add(
            (number, "first", 2),
            nothing,
            0.1,
            1,
            needs=[need(("af", s), first, s, 2, 0, True) for s in (1, 3)],
            sends=[*spread(2), exchange(2, 0)],
        )
        for a in (0, 3, 1, 2):
            for s in (1, 3):
                b = OPPOSITE[s]
                add(
                    (number, "second", a, s),
                    nothing,
                    0.1,
                    1,
                    needs=[need(("b", a, s), second, s, a, b)],
                    sends=[half(("bf", a, s), second, s, a, b), exchange(a, b)],
                )
            add(
                (number, "second", a, 2),
                nothing,
                0.1,
                1,
                needs=[need(("bf", a, s), second, s, a, 2, True) for s in (1, 3)],
                sends=[exchange(a, 2)],
            )

        def settled(dy):
            needs = []
            for dz in range(RING):
                a, b = (dz, dy) if first == "z" else (dy, dz)

                def refs(a=a, b=b):
                    return held(a, b, other=True), env.partner

                needs.append(((number, "x", a, b), refs))
            return needs

        return settled

    settled = [gather(("g", i), *part) for i, part in enumerate(GATHER_PARTS)]

    chunk_bytes = 2 * block * rows * 2

    def turn_refs(i):
        def refs():
            span = pl.ds(2 * env.chunk(*CHUNKS[i]), 2)
            return (
                env.turned.at[span, 1 - env.core],
                env.turned_other.at[span],
                env.partner,
            )

        return refs

    def turn_need(i):
        def refs():
            return turn_refs(i)()[1], env.partner

        return ("t", i), refs

    add(
        "cot",
        lambda: env.start_rest(),
        0.4,
        0,
        sends=[
            (
                "cot",
                "c",
                rows * WIDTH * 2,
                lambda: (env.cotangent, env.cot.at[1], env.partner),
            )
        ],
    )
    add("square", lambda: env.square(), 2.5, 2, after=["cot"])
    for i in range(len(CHUNKS)):
        add(
            ("turn", i),
            lambda i=i: env.turn(env.chunk(*CHUNKS[i])),
            0.4,
            0.5,
            after=["square"] + ([("turn", i - 1)] if i else []),
            sends=[(("t", i), "c", chunk_bytes, turn_refs(i))],
        )
        needs = [turn_need(i)]
        if i == 0:
            needs.append(("cot", lambda: (env.cot.at[1], env.partner)))
        add(
            ("product", i),
            lambda i=i: env.multiply(env.chunk(*CHUNKS[i])),
            0.15,
            2.5,
            needs=needs,
            after=[("product", i - 1)] if i else [],
        )

    def scatter(number, lo, hi, first):
        size = hi - lo
        second = "y" if first == "z" else "z"
        halves = {1: pl.ds(0, size // 2), 3: pl.ds(size // 2, size // 2)}
        index = {1: 0, 3: 1}
        start = {1: lo, 3: lo + size // 2}
        whole_size, half_size = size * WIDTH * 2, size * WIDTH
        bf16, f32 = jnp.bfloat16, jnp.float32

        def offset(a, b):
            return (b, a) if first == "z" else (a, b)

        def target(axis, s):
            return env.device(0, s) if axis == "z" else env.device(s, 0)

        def mine(a, b, s=None):
            span = pl.ds(lo, size) if s is None else pl.ds(start[s], size // 2)
            return env.part[env.chip[offset(a, b)], span, :]

        def bufs():
            return env.scatter[number[1]]

        def far_refs(b, s):
            r = bufs()
            return (
                r.far_out.at[b, halves[s]],
                r.far_in.at[b, halves[s]],
                target(first, s),
            )

        def near_refs(b, s):
            r = bufs()
            return r.near_out.at[index[s], b], r.near_in.at[index[s], b], target(first, s)

        def far2_refs(s):
            r = bufs()
            return r.far2_out.at[halves[s]], r.far2_in.at[halves[s]], target(second, s)

        def near2_refs(s):
            r = bufs()
            return r.near2_out.at[index[s]], r.near2_in.at[index[s]], target(second, s)

        def need(key, fn, *args):
            return (number, *key), lambda: fn(*args)[1:]

        def far(b):
            for s in (1, 3):
                bufs().far_out[b, halves[s], :] = mine(2, b, s).astype(bf16)

        def near(b, s):
            r, i = bufs(), index[s]
            r.near_out[i, b, halves[OPPOSITE[s]], :] = mine(s, b, OPPOSITE[s]).astype(bf16)
            r.near_out[i, b, halves[s], :] = (
                mine(s, b, s) + r.far_in[b, halves[s], :].astype(f32)
            ).astype(bf16)

        def gathered(b):
            r = bufs()
            r.total[b] = (
                mine(0, b) + r.near_in[0, b].astype(f32) + r.near_in[1, b].astype(f32)
            )

        def far2():
            r = bufs()
            for s in (1, 3):
                r.far2_out[halves[s], :] = r.total[2, halves[s], :].astype(bf16)

        def near2(s):
            r, i, o = bufs(), index[s], halves[OPPOSITE[s]]
            r.near2_out[i, o, :] = r.total[s, o, :].astype(bf16)
            r.near2_out[i, halves[s], :] = (
                r.total[s, halves[s], :] + r.far2_in[halves[s], :].astype(f32)
            ).astype(bf16)

        def final():
            r = bufs()
            env.weight_out[pl.ds(lo, size), :] = (
                r.total[0] + r.near2_in[0].astype(f32) + r.near2_in[1].astype(f32)
            )

        for b in (2, 1, 3, 0):
            add(
                (number, "far", b),
                functools.partial(far, b),
                0.15,
                2,
                after=product(*offset(2, b)),
                sends=[
                    (
                        (number, "f", b, s),
                        first + str(s),
                        half_size,
                        functools.partial(far_refs, b, s),
                    )
                    for s in (1, 3)
                ],
            )
            for s in (1, 3):
                add(
                    (number, "near", b, s),
                    functools.partial(near, b, s),
                    0.2,
                    2,
                    needs=[need(("f", b, s), far_refs, b, s)],
                    after=product(*offset(s, b)) + [(number, "far", b)],
                    sends=[
                        (
                            (number, "n", b, s),
                            first + str(s),
                            whole_size,
                            functools.partial(near_refs, b, s),
                        )
                    ],
                )
            add(
                (number, "sum", b),
                functools.partial(gathered, b),
                0.2,
                2,
                needs=[need(("n", b, s), near_refs, b, s) for s in (1, 3)],
                after=product(*offset(0, b)),
            )
        add(
            (number, "far2"),
            far2,
            0.1,
            2,
            after=[(number, "sum", 2)],
            sends=[
                (
                    (number, "f2", s),
                    second + str(s),
                    half_size,
                    functools.partial(far2_refs, s),
                )
                for s in (1, 3)
            ],
        )
        for s in (1, 3):
            add(
                (number, "near2", s),
                functools.partial(near2, s),
                0.2,
                2,
                needs=[need(("f2", s), far2_refs, s)],
                after=[(number, "sum", s)],
                sends=[
                    (
                        (number, "n2", s),
                        second + str(s),
                        whole_size,
                        functools.partial(near2_refs, s),
                    )
                ],
            )
        add(
            (number, "final"),
            final,
            0.3,
            2,
            needs=[need(("n2", s), near2_refs, s) for s in (1, 3)],
            after=[(number, "sum", 0)],
        )

    for i, part in enumerate(SCATTER_PARTS):
        scatter(("s", i), *part)

    def x_refs(d):
        return env.x_in.at[env.x], env.x_in.at[env.x], env.beside_x(d)

    def x_need(d):
        return ("ox", d), lambda: (
            env.x_in.at[lax.rem(env.x + RING - d, RING)],
            env.beside_x(d),
        )

    add(
        "outer",
        lambda: env.differ(),
        0.5,
        2.2,
        after=["square"],
        sends=[
            (("ox", d), "x" + str(d), 65536, functools.partial(x_refs, d)) for d in (1, 2, 3)
        ],
    )
    add(
        "outer2",
        lambda: env.add_x(),
        0.5,
        4,
        needs=[x_need(d) for d in (1, 2, 3)],
        sends=[("oz", "z1", 65536, lambda: (env.z_out, env.z_in, env.beside_low))],
    )
    add(
        "outer3",
        lambda: env.update(),
        0.8,
        4,
        needs=[("oz", lambda: (env.z_in, env.beside_low))],
    )

    add("own", lambda: env.own_copy.wait(), 0.0, 2, after=["square"])
    gain_bytes = features // RING * 4
    for dy in (0, 1, 3, 2):
        add(
            ("project", dy),
            functools.partial(lambda dy: env.project(dy), dy),
            1.0,
            2.8,
            needs=[n for fn in settled for n in fn(dy)],
            after=["own"],
            sends=[
                (
                    ("gc", dy),
                    "c",
                    gain_bytes,
                    lambda dy=dy: (env.gain_own.at[dy], env.gain_core.at[dy], env.partner),
                )
            ],
        )
        if dy:
            sends = [
                (
                    ("gy", dy),
                    "y" + str(dy) if dy != 2 else "y1",
                    gain_bytes,
                    lambda dy=dy: (
                        env.gain_chip.at[dy],
                        env.gain_y.at[dy],
                        env.device(dy, 0),
                    ),
                )
            ]
        else:
            sends = []
        add(
            ("gain", dy),
            functools.partial(lambda dy: env.gain_chip_sum(dy), dy),
            0.1,
            1,
            needs=[
                (("gc", dy), lambda dy=dy: (env.gain_core.at[dy], env.partner))
            ],
            after=[("project", dy)],
            sends=sends,
        )
    add(
        "gain y",
        lambda: env.gain_y_sum(),
        0.1,
        1,
        needs=[
            (("gy", d), lambda d=d: (env.gain_y.at[d], env.device(d, 0))) for d in (1, 2, 3)
        ],
        after=[("gain", 0)],
        sends=[
            (
                ("gz", d),
                "z" + str(d) if d != 2 else "z1",
                gain_bytes,
                lambda d=d: (env.gain_z.at[0], env.gain_z.at[d], env.device(0, d)),
            )
            for d in (1, 2, 3)
        ],
    )
    add(
        "gain z",
        lambda: env.gain_z_sum(),
        0.2,
        3,
        needs=[
            (("gz", d), lambda d=d: (env.gain_z.at[d], env.device(0, d))) for d in (1, 2, 3)
        ],
    )
    add(
        "finish",
        lambda: env.finish(),
        2.0,
        2.9,
        after=[("project", dy) for dy in range(RING)],
    )
    return events


def kernel(
    plan,
    tokens,
    gain_all,
    weight,
    cotangent,
    replica_part,
    anchor,
    velocity,
    chosen,
    token_out,
    weight_out,
    gain_out,
    param_out,
    momentum_out,
    gain,
    turned,
    turned_other,
    cot,
    full,
    part,
    scaled,
    inverse,
    projected,
    gain_own,
    gain_core,
    gain_chip,
    gain_y,
    gain_z,
    replica_in,
    anchor_in,
    velocity_in,
    x_in,
    z_out,
    z_in,
    *rest,
):
    buffers, (send_sem, recv_sem, local_sem) = rest[:-3], rest[-3:]
    rows, features = token_out.shape
    block = weight.shape[0]
    f32, bf16 = jnp.float32, jnp.bfloat16
    tok = token_out

    worker = lax.axis_index("worker")
    place = lax.axis_index("fsdp")
    core = lax.rem(place, 2)
    z = lax.rem(place // 2, RING)
    y = place // (2 * RING)
    x, low = worker // 2, lax.rem(worker, 2)

    env = types.SimpleNamespace(
        core=core,
        x=x,
        weight=weight,
        cotangent=cotangent,
        cot=cot,
        turned=turned,
        turned_other=turned_other,
        part=part,
        x_in=x_in,
        z_out=z_out,
        z_in=z_in,
        weight_out=weight_out,
        gain_own=gain_own,
        gain_core=gain_core,
        gain_chip=gain_chip,
        gain_y=gain_y,
        gain_z=gain_z,
    )
    env.chip = {
        (dy, dz): lax.rem(y + dy, RING) * RING + lax.rem(z + dz, RING)
        for dy in range(RING)
        for dz in range(RING)
    }
    env.device = lambda dy, dz: {"fsdp": 2 * env.chip[dy, dz] + core}
    env.partner = {"fsdp": place + 1 - 2 * core}
    env.beside_x = lambda d: {"worker": lax.rem(x + d, RING) * 2 + low}
    env.beside_low = {"worker": x * 2 + 1 - low}
    env.chunk = lambda dy, far: lax.rem(y + dy, RING) * 2 + (
        1 - z // 2 if far else z // 2
    )
    names = ["far_out", "far_in", "near_out", "near_in"]
    names += ["far2_out", "far2_in", "near2_out", "near2_in", "total"]
    env.scatter = [
        types.SimpleNamespace(**dict(zip(names, buffers[9 * i : 9 * i + 9])))
        for i in range(len(SCATTER_PARTS))
    ]

    def slot(dy, dz, which, lo, hi):
        start = (2 * env.chip[dy, dz] + which) * block + lo
        return full.at[pl.ds(pl.multiple_of(start, 16), hi - lo)]

    env.slot = slot

    half_rows = rows // 2
    token_copies = []
    for i in range(2):
        span = pl.ds(i * half_rows, half_rows)
        token_copies.append(
            pltpu.make_async_copy(tokens.at[span], tok.at[span], local_sem.at[i])
        )
    cot_copy = pltpu.make_async_copy(cotangent, cot.at[0], local_sem.at[2])
    gain_copy = pltpu.make_async_copy(gain_all, gain, local_sem.at[7])
    own = pl.ds(pl.multiple_of(place * block, 16), block)
    env.own_copy = pltpu.make_async_copy(weight, full.at[own], local_sem.at[3])
    fragment_copies = [
        pltpu.make_async_copy(src, dst, local_sem.at[4 + i])
        for i, (src, dst) in enumerate(
            ((replica_part, replica_in), (anchor, anchor_in), (velocity, velocity_in))
        )
    ]
    greeted = [env.partner, env.beside_low]
    greeted += [env.beside_x(d) for d in (1, 2, 3)]
    greeted += [env.device(d, 0) for d in (1, 2, 3)]
    greeted += [env.device(0, d) for d in (1, 2, 3)]
    barrier = pltpu.get_barrier_semaphore()
    for target in greeted:
        pl.semaphore_signal(barrier, inc=1, device_id=target, device_id_type=MESH)
    for c in token_copies:
        c.start()
    pl.semaphore_wait(barrier, len(greeted))

    def start_rest():
        for c in (gain_copy, cot_copy, env.own_copy, *fragment_copies):
            c.start()

    def square():
        projected[...] = jnp.zeros_like(projected)
        for c in (gain_copy, cot_copy):
            c.wait()
        for i in range(2):
            token_copies[i].wait()
            here = pl.ds(i * half_rows, half_rows)

            def step(j, total):
                wide = tok[here, pl.ds(pl.multiple_of(j * 256, 128), 256)].astype(f32)
                wide = wide * wide
                return total + wide[:, :128] + wide[:, 128:]

            total = lax.fori_loop(
                0, features // 256, step, jnp.zeros((half_rows, 128), f32)
            )
            inv = lax.rsqrt(jnp.sum(total, axis=1, keepdims=True) / features + EPSILON)
            inverse[here, :] = jnp.broadcast_to(inv, (half_rows, 128))

    def turn(j):
        width = 4 * block
        cols = pl.ds(pl.multiple_of(j * width, 128), width)
        for i in range(2):
            here = pl.ds(i * half_rows, half_rows)
            inv = inverse[here, 0:1]
            normed = (tok[here, cols].astype(f32) * inv * gain[:, cols]).astype(bf16)
            flipped = normed.T
            for b in range(4):
                turned[2 * j + b // 2, b % 2, :, here] = flipped[
                    b * block : (b + 1) * block
                ]
        for k in range(2):
            part[2 * j + k] = jnp.dot(
                turned[2 * j + k, core], cot[0], preferred_element_type=f32
            )

    def multiply(j):
        for k in range(2):
            part[2 * j + k] += jnp.dot(
                turned_other[2 * j + k], cot[1], preferred_element_type=f32
            )

    span = features // RING
    width = span // 2

    def project(dy):
        start = pl.multiple_of(lax.rem(y + dy, RING) * span, 128)

        @pl.loop(0, 2)
        def _(i):
            here = pl.ds(pl.multiple_of(start + i * width, 128), width)
            d = lax.dot_general(cot[0], full[here, :], NT, preferred_element_type=f32)
            scale = gain[:, here]
            scaled[:, here] = d * scale
            both = d * tok[:, here].astype(f32)
            with_gain = both * scale
            total = with_gain[:, :128]
            for k in range(1, width // 128):
                total = total + with_gain[:, k * 128 : (k + 1) * 128]
            projected[...] += total
            inv = inverse[...]
            for k in range(width // 128):
                cols = pl.ds(pl.multiple_of(i * width + k * 128, 128), 128)
                gain_own[dy, :, cols] = jnp.sum(
                    both[:, k * 128 : (k + 1) * 128] * inv, axis=0, keepdims=True
                )

    def finish():
        step = 64

        @pl.loop(0, rows // step)
        def _(i):
            here = pl.ds(pl.multiple_of(i * step, step), step)
            inv = inverse[here, 0:1]
            mean = jnp.sum(projected[here, :], axis=1, keepdims=True) / features
            back = inv * inv * inv * mean

            for j in range(features // 1024):
                cols = pl.ds(j * 1024, 1024)
                wide = tok[here, cols].astype(f32)
                tok[here, cols] = (inv * scaled[here, cols] - wide * back).astype(bf16)

    def gain_chip_sum(dy):
        total = gain_own[dy] + gain_core[dy]
        if dy:
            gain_chip[dy] = total
        else:
            gain_y[0] = total

    def gain_y_sum():
        gain_z[0] = gain_y[0] + gain_y[1] + gain_y[2] + gain_y[3]

    def gain_z_sum():
        total = gain_z[0] + gain_z[1] + gain_z[2] + gain_z[3]
        which = 2 * z + core
        chosen_part = total[:, :block]
        for i in range(1, 2 * RING):
            chosen_part = jnp.where(
                which == i, total[:, i * block : (i + 1) * block], chosen_part
            )
        gain_out[...] = chosen_part

    def differ():
        for c in fragment_copies:
            c.wait()
        index = chosen[0]
        x_in[x] = anchor_in[pl.ds(index, 1), :] - replica_in[pl.ds(index, 1), :]

    def add_x():
        z_out[...] = x_in[0] + x_in[1] + x_in[2] + x_in[3]

    def update():
        index = chosen[0]
        pseudo = (z_out[...] + z_in[...]) / 8
        momentum = MOMENTUM * velocity_in[pl.ds(index, 1), :] + pseudo
        momentum_out[...] = momentum
        param_out[...] = anchor_in[pl.ds(index, 1), :] - OUTER_RATE * (
            pseudo + MOMENTUM * momentum
        )

    for fn in (
        start_rest,
        square,
        turn,
        multiply,
        project,
        finish,
        gain_chip_sum,
        gain_y_sum,
        gain_z_sum,
        differ,
        add_x,
        update,
    ):
        setattr(env, fn.__name__, fn)

    order = plan(env)
    numbers = {}
    for e in order:
        for key, _, _, _ in e.sends:
            numbers[key] = len(numbers)

    def copy(key, src, dst, target):
        return pltpu.make_async_remote_copy(
            src_ref=src,
            dst_ref=dst,
            send_sem=send_sem.at[numbers[key]],
            recv_sem=recv_sem.at[numbers[key]],
            device_id=target,
            device_id_type=MESH,
        )

    sent = []
    for e in order:
        for key, refs in e.needs:
            dst, target = refs()
            copy(key, dst, dst, target).wait_recv()
        e.body()
        for key, _, _, refs in e.sends:
            c = copy(key, *refs())
            c.start()
            sent.append(c)
    for c in sent:
        c.wait_send()


def write_out(*refs):
    count = len(refs) // 2
    sem = refs[-1]
    copies = [
        pltpu.make_async_copy(refs[i], refs[count + i], sem.at[i]) for i in range(count)
    ]
    for c in copies:
        c.start()
    for c in copies:
        c.wait()


def local(
    tokens,
    norm_gain,
    value_weight,
    value_cotangent,
    local_fragments,
    global_fragments,
    outer_velocity,
    fragment_index,
):
    _, rows, features = tokens.shape
    _, block, values = value_weight.shape
    blocks = RING * RING
    fragments, length = global_fragments.shape
    span = features // RING
    vmem = pltpu.VMEM
    bf16, f32 = jnp.bfloat16, jnp.float32

    def plan(env):
        events = build(env, rows, features, block)
        return [events[i] for i in ORDER]

    sems = sum(len(e.sends) for e in plan(None))
    scratch = [
        vmem((1, features), f32),
        vmem((blocks, 2, block, rows), bf16),
        vmem((blocks, block, rows), bf16),
        vmem((2, rows, values), bf16),
        vmem((features, values), bf16),
        vmem((blocks, block, values), f32),
        vmem((rows, features), f32),
        vmem((rows, 128), f32),
        vmem((rows, 128), f32),
        vmem((RING, 1, span), f32),
        vmem((RING, 1, span), f32),
        vmem((RING, 1, span), f32),
        vmem((RING, 1, span), f32),
        vmem((RING, 1, span), f32),
        vmem((fragments, length), f32),
        vmem((fragments, length), f32),
        vmem((fragments, length), f32),
        vmem((RING, 1, length), f32),
        vmem((1, length), f32),
        vmem((1, length), f32),
    ]
    for lo, hi, _ in SCATTER_PARTS:
        size = hi - lo
        scratch += [
            vmem((RING, size, values), bf16),
            vmem((RING, size, values), bf16),
            vmem((2, RING, size, values), bf16),
            vmem((2, RING, size, values), bf16),
            vmem((size, values), bf16),
            vmem((size, values), bf16),
            vmem((2, size, values), bf16),
            vmem((2, size, values), bf16),
            vmem((RING, size, values), f32),
        ]
    scratch += [
        pltpu.SemaphoreType.DMA((sems,)),
        pltpu.SemaphoreType.DMA((sems,)),
        pltpu.SemaphoreType.DMA((8,)),
    ]
    in_vmem = pl.BlockSpec(memory_space=pltpu.VMEM)
    in_hbm = pl.BlockSpec(memory_space=pltpu.HBM)
    shapes = [
        ((rows, features), bf16),
        ((block, values), f32),
        ((1, block), f32),
        ((1, length), f32),
        ((1, length), f32),
    ]
    keep = functools.partial(pltpu.with_memory_space_constraint, memory_space=pltpu.HBM)
    results = pl.pallas_call(
        functools.partial(kernel, plan),
        out_shape=[vmem(*s) for s in shapes],
        in_specs=[in_hbm] * 7 + [pl.BlockSpec(memory_space=pltpu.SMEM)],
        out_specs=[in_vmem] * len(shapes),
        scratch_shapes=scratch,
        compiler_params=pltpu.CompilerParams(
            collective_id=0, has_side_effects=True, vmem_limit_bytes=42 * 2**20
        ),
        cost_estimate=pl.CostEstimate(
            flops=4 * rows * features * values, bytes_accessed=2**24, transcendentals=0
        ),
    )(
        keep(tokens[0]),
        keep(norm_gain),
        keep(value_weight[0]),
        keep(value_cotangent[0]),
        keep(local_fragments[0]),
        keep(global_fragments),
        keep(outer_velocity),
        fragment_index,
    )
    results = [pltpu.with_memory_space_constraint(r, pltpu.VMEM) for r in results]
    token_grad, weight_grad, gain_grad, param, momentum = pl.pallas_call(
        write_out,
        out_shape=[jax.ShapeDtypeStruct(*s) for s in shapes],
        in_specs=[in_vmem] * len(shapes),
        out_specs=[in_hbm] * len(shapes),
        scratch_shapes=[pltpu.SemaphoreType.DMA((len(shapes),))],
        compiler_params=pltpu.CompilerParams(vmem_limit_bytes=2**20),
    )(*results)
    return (
        token_grad[None],
        weight_grad[None],
        gain_grad,
        param.reshape(-1),
        momentum.reshape(-1),
    )


def solution(mesh):
    placed = (
        P("worker", "fsdp", None),
        P("worker", None),
        P("worker", "fsdp", None),
        P("worker", "fsdp", None),
        P("worker", None, "fsdp"),
        P(None, "fsdp"),
        P(None, "fsdp"),
        P(),
    )
    return jax.shard_map(
        local,
        mesh=mesh,
        in_specs=placed,
        out_specs=(
            P("worker", "fsdp", None),
            P("worker", "fsdp", None),
            P("worker", "fsdp"),
            P("fsdp"),
            P("fsdp"),
        ),
        check_vma=False,
    )
```

time: 359 us -> 72.5 us (0.20)
  waiting for transfers between devices: 306 us -> 0 us
  Pallas kernels: 0 us -> 70.4 us
  matrix products: 19 us -> 0 us
  between operations: 15.9 us -> 1.29 us
  other arithmetic: 12.8 us -> 0 us
  local copies, waits for them, and re-layouts: 5.2 us -> 0 us
    reduce_scatter x1 -> x0, waiting for transfers between devices: 154 us -> none  [local(): lax.psum_scatter(lax.dot_general(normed, upstream, (((0,), (0,)), ((), ()...]
    unnamed x5 -> x0, waiting for transfers between devices: 77.3 us -> none
    all_gather x1 -> x0, waiting for transfers between devices: 74.1 us -> none  [local(): lax.all_gather(value_weight, 'fsdp', axis=1, tiled=True)[0]]
    pallas_call x0 -> x2, Pallas kernels: none -> 70.4 us  [the longest x1 68.3 us: local(): pl.pallas_call(functools.partial(kernel, plan), out_shape=[vmem(*s) for s...]
    dot_general x2 -> x0, matrix products: 19 us -> none  [the longest x1 9.56 us: local(): lax.dot_general(upstream, lax.all_gather(value_weight, 'fsdp', axis=1, ti...]
    broadcast_in_dim x1 -> x0, other arithmetic: 6.69 us -> none  [local(): (inverse * (scaled - widened * inverse * inverse * projected)).astype(jnp...]
    unnamed x8 -> x0, local copies, waits for them, and re-layouts: 4.05 us -> none
  transfers between devices with their start and end apart: 4 -> 0, of which waited for: 3 -> 0; matrix products, arithmetic and copies ran while one was open for 10% -> 0% of each run, Pallas kernels for 0% -> 0%
where the time goes in v2:
time: 72.5 us; the launch traced here: 71.7 us
  Pallas kernels  70.4 us (97%)
  between operations  1.29 us (2%)
    pallas_call x1, Pallas kernels, local(): pl.pallas_call(functools.partial(kernel, plan), out_shape=[vmem(*s) for s...  68.3 us
    pallas_call x1, Pallas kernels, local(): pl.pallas_call(write_out, out_shape=[jax.ShapeDtypeStruct(*s) for s in sh...  2.06 us

profile of v2, /device:TPU:6, one launch (start us, length us, event | category | flops | bytes accessed | tf_op | source)
XLA Modules:
  0.0 71.7 jit_solution(16650988240134612967)
XLA Ops:
  1.3 68.3 %shard_map.119 = (bf16[256,7168]{1,0:T(8,128)(2,1)S(1)}, f32[224,512]{1,0:T(8,128)S(1)}, f32[1,224]{1,0:T(1,128)S(1)}, f32[1,16384]{1,0:T(1,128)S(1)}, f32[1,16384]{1,0:T(1,128)S(1)}) custom-call(bf16[256,7168]{1,0:T(8,128)(2,1)} %bitcast.8, f32[1,7168]{1,0:T(1,128)} %gain_all.1, bf16[224,512]{1,0:T(8,128)(2,1)} %bitcast.13, bf16[256,512]{1,0:T(8,128)(2,1)} %bitcast.12, ...), custom_call_target="tpu_custom_call" | custom-call | flops 3758096384 | bytes 16777216 | tf_op jit(solution)/shard_map/pallas_call | solution.py:881
  69.6 2.1 %shard_map.120 = (bf16[256,7168]{1,0:T(8,128)(2,1)}, f32[224,512]{1,0:T(8,128)}, f32[1,224]{1,0:T(1,128)}, f32[1,16384]{1,0:T(1,128)}, f32[1,16384]{1,0:T(1,128)}) custom-call(bf16[256,7168]{1,0:T(8,128)(2,1)S(1)} %get-tuple-element.15.refs_0_, f32[224,512]{1,0:T(8,128)S(1)} %get-tuple-element.16.refs_1_, f32[1,224]{1,0:T(1,128)S(1)} %get-tuple-element.17.refs_2_, ...), custom_call_target="tpu_custom_call" | custom-call | tf_op jit(solution)/shard_map/pallas_call | solution.py:904

commit v3 on v2

--- a/solution.py
+++ b/solution.py
@@ -14,17 +14,17 @@
 MESH = pl.DeviceIdType.MESH
 RING = 4
 NT = (((1,), (1,)), ((), ()))
-GATHER_PARTS = ((0, 64, "z"), (64, 128, "z"), (128, 224, "z"))
-SCATTER_PARTS = ((0, 64, "y"), (64, 128, "y"), (128, 224, "z"))
+GATHER_PARTS = ((0, 224, "z"),)
+SCATTER_PARTS = ((0, 64, "y"), (64, 144, "y"), (144, 224, "z"))
 WIDTH = 512
+LAG = 12
+PIECES = 4
 ORDER = (
-    0, 32, 16, 48, 49, 4, 50, 52, 54, 5, 1, 2, 20, 21, 51, 106, 86, 66, 56, 6, 58, 33, 8, 34,
-    126, 11, 10, 22, 18, 17, 129, 36, 53, 3, 67, 110, 55, 114, 68, 127, 57, 59, 118, 90, 42, 39,
-    35, 87, 12, 107, 19, 26, 27, 70, 108, 94, 24, 74, 43, 37, 13, 14, 88, 40, 23, 69, 82, 7, 60,
-    62, 64, 128, 46, 61, 112, 63, 115, 30, 45, 65, 72, 111, 132, 116, 76, 29, 28, 44, 71, 109,
-    122, 38, 95, 75, 96, 15, 133, 120, 25, 89, 102, 9, 41, 92, 119, 47, 91, 134, 31, 73, 83,
-    135, 98, 136, 113, 123, 78, 137, 77, 84, 97, 117, 124, 93, 103, 99, 100, 104, 130, 80, 121,
-    79, 131, 138, 140, 101, 125, 81, 85, 105, 139,
+    0, 16, 17, 18, 20, 22, 24, 19, 34, 54, 21, 78, 23, 94, 25, 58, 82, 38, 42, 26, 28, 4, 5, 35,
+    62, 98, 27, 29, 39, 36, 55, 95, 56, 2, 1, 30, 31, 57, 84, 79, 74, 3, 32, 70, 40, 11, 96, 37,
+    10, 86, 50, 6, 7, 83, 75, 8, 76, 99, 14, 97, 64, 33, 87, 13, 88, 63, 43, 101, 102, 41, 80,
+    51, 12, 85, 60, 59, 103, 46, 44, 66, 9, 15, 65, 72, 105, 77, 90, 100, 61, 71, 106, 104, 48,
+    47, 45, 52, 67, 68, 81, 92, 89, 91, 107, 49, 109, 69, 73, 53, 108, 93,
 )
 OPPOSITE = {1: 3, 3: 1, 2: 2}
 CHUNKS = ((2, 1), (1, 1), (3, 1), (2, 0), (0, 1), (1, 0), (3, 0), (0, 0))
@@ -52,10 +52,11 @@
         return [("product", chunk_of[dy, s]) for s in sides]
 
     def gather(number, lo, hi, first):
-        mid = (lo + hi) // 2
+        mid = lo + (hi - lo) // 32 * 16
         halves = {1: (lo, mid), 3: (mid, hi)}
         second = "y" if first == "z" else "z"
-        full_size, half_size = (hi - lo) * WIDTH * 2, (hi - lo) * WIDTH
+        full_size = (hi - lo) * WIDTH * 2
+        half_size = {1: (mid - lo) * WIDTH * 2, 3: (hi - mid) * WIDTH * 2}
 
         def offset(a, b):
             return (b, a) if first == "z" else (a, b)
@@ -80,7 +81,7 @@
                 here = held(a, b, halves[s])
                 return here, here, target(axis, s)
 
-            return (number, *key), axis + str(s), half_size, refs
+            return (number, *key), axis + str(s), half_size[s], refs
 
         def exchange(a, b, own=False):
             def refs():
@@ -219,10 +220,12 @@
     def scatter(number, lo, hi, first):
         size = hi - lo
         second = "y" if first == "z" else "z"
-        halves = {1: pl.ds(0, size // 2), 3: pl.ds(size // 2, size // 2)}
+        mid = size // 32 * 16
+        halves = {1: pl.ds(0, mid), 3: pl.ds(mid, size - mid)}
         index = {1: 0, 3: 1}
-        start = {1: lo, 3: lo + size // 2}
-        whole_size, half_size = size * WIDTH * 2, size * WIDTH
+        spans = {1: pl.ds(lo, mid), 3: pl.ds(lo + mid, size - mid)}
+        whole_size = size * WIDTH * 2
+        half_size = {1: mid * WIDTH * 2, 3: (size - mid) * WIDTH * 2}
         bf16, f32 = jnp.bfloat16, jnp.float32
 
         def offset(a, b):
@@ -232,7 +235,7 @@
             return env.device(0, s) if axis == "z" else env.device(s, 0)
 
         def mine(a, b, s=None):
-            span = pl.ds(lo, size) if s is None else pl.ds(start[s], size // 2)
+            span = pl.ds(lo, size) if s is None else spans[s]
             return env.part[env.chip[offset(a, b)], span, :]
 
         def bufs():
@@ -307,7 +310,7 @@
                     (
                         (number, "f", b, s),
                         first + str(s),
-                        half_size,
+                        half_size[s],
                         functools.partial(far_refs, b, s),
                     )
                     for s in (1, 3)
@@ -317,7 +320,7 @@
                 add(
                     (number, "near", b, s),
                     functools.partial(near, b, s),
-                    0.2,
+                    0.12,
                     2,
                     needs=[need(("f", b, s), far_refs, b, s)],
                     after=product(*offset(s, b)) + [(number, "far", b)],
@@ -348,7 +351,7 @@
                 (
                     (number, "f2", s),
                     second + str(s),
-                    half_size,
+                    half_size[s],
                     functools.partial(far2_refs, s),
                 )
                 for s in (1, 3)
@@ -383,14 +386,25 @@
     for i, part in enumerate(SCATTER_PARTS):
         scatter(("s", i), *part)
 
+    def x_from(d):
+        return lax.rem(env.x + RING - d, RING)
+
     def x_refs(d):
-        return env.x_in.at[env.x], env.x_in.at[env.x], env.beside_x(d)
+        return env.quarter(lax.rem(env.x + d, RING)), env.x_in.at[env.x], env.beside_x(d)
 
     def x_need(d):
-        return ("ox", d), lambda: (
-            env.x_in.at[lax.rem(env.x + RING - d, RING)],
-            env.beside_x(d),
-        )
+        return ("ox", d), lambda: (env.x_in.at[x_from(d)], env.beside_x(d))
+
+    def all_refs(d):
+        return env.total.at[env.x], env.total.at[env.x], env.beside_x(d)
+
+    def all_need(d):
+        return ("oa", d), lambda: (env.total.at[x_from(d)], env.beside_x(d))
+
+    def to_x(key, refs):
+        return [
+            ((key, d), "x" + str(d), 16384, functools.partial(refs, d)) for d in (1, 2, 3)
+        ]
 
     add(
         "outer",
@@ -398,24 +412,30 @@
         0.5,
         2.2,
         after=["square"],
-        sends=[
-            (("ox", d), "x" + str(d), 65536, functools.partial(x_refs, d)) for d in (1, 2, 3)
-        ],
+        sends=to_x("ox", x_refs),
     )
     add(
         "outer2",
         lambda: env.add_x(),
-        0.5,
+        0.2,
         4,
         needs=[x_need(d) for d in (1, 2, 3)],
-        sends=[("oz", "z1", 65536, lambda: (env.z_out, env.z_in, env.beside_low))],
+        sends=[("oz", "z1", 8192, lambda: (env.z_out, env.z_in, env.beside_low))],
     )
     add(
         "outer3",
-        lambda: env.update(),
-        0.8,
+        lambda: env.add_z(),
+        0.1,
         4,
         needs=[("oz", lambda: (env.z_in, env.beside_low))],
+        sends=to_x("oa", all_refs),
+    )
+    add(
+        "outer4",
+        lambda: env.update(),
+        0.6,
+        4,
+        needs=[all_need(d) for d in (1, 2, 3)],
     )
 
     add("own", lambda: env.own_copy.wait(), 0.0, 2, after=["square"])
@@ -533,9 +553,11 @@
     replica_in,
     anchor_in,
     velocity_in,
+    difference,
     x_in,
     z_out,
     z_in,
+    total,
     *rest,
 ):
     buffers, (send_sem, recv_sem, local_sem) = rest[:-3], rest[-3:]
@@ -563,6 +585,7 @@
         x_in=x_in,
         z_out=z_out,
         z_in=z_in,
+        total=total,
         weight_out=weight_out,
         gain_own=gain_own,
         gain_core=gain_core,
@@ -612,10 +635,10 @@
             ((replica_part, replica_in), (anchor, anchor_in), (velocity, velocity_in))
         )
     ]
-    greeted = [env.partner, env.beside_low]
+    greeted = [env.device(0, d) for d in (1, 3, 2)]
+    greeted += [env.device(d, 0) for d in (1, 3, 2)]
+    greeted += [env.partner, env.beside_low]
     greeted += [env.beside_x(d) for d in (1, 2, 3)]
-    greeted += [env.device(d, 0) for d in (1, 2, 3)]
-    greeted += [env.device(0, d) for d in (1, 2, 3)]
     barrier = pltpu.get_barrier_semaphore()
     for target in greeted:
         pl.semaphore_signal(barrier, inc=1, device_id=target, device_id_type=MESH)
@@ -729,23 +752,36 @@
             )
         gain_out[...] = chosen_part
 
+    piece = difference.shape[1] // RING
+
+    def quarter(i):
+        return difference.at[:, pl.ds(pl.multiple_of(i * piece, 128), piece)]
+
+    env.quarter = quarter
+
     def differ():
         for c in fragment_copies:
             c.wait()
         index = chosen[0]
-        x_in[x] = anchor_in[pl.ds(index, 1), :] - replica_in[pl.ds(index, 1), :]
+        difference[...] = anchor_in[pl.ds(index, 1), :] - replica_in[pl.ds(index, 1), :]
+        x_in[x] = quarter(x)[...]
 
     def add_x():
         z_out[...] = x_in[0] + x_in[1] + x_in[2] + x_in[3]
 
+    def add_z():
+        total[x] = z_out[...] + z_in[...]
+
     def update():
         index = chosen[0]
-        pseudo = (z_out[...] + z_in[...]) / 8
-        momentum = MOMENTUM * velocity_in[pl.ds(index, 1), :] + pseudo
-        momentum_out[...] = momentum
-        param_out[...] = anchor_in[pl.ds(index, 1), :] - OUTER_RATE * (
-            pseudo + MOMENTUM * momentum
-        )
+        for i in range(RING):
+            here = pl.ds(i * piece, piece)
+            pseudo = total[i] / 8
+            momentum = MOMENTUM * velocity_in[pl.ds(index, 1), here] + pseudo
+            momentum_out[:, here] = momentum
+            param_out[:, here] = anchor_in[pl.ds(index, 1), here] - OUTER_RATE * (
+                pseudo + MOMENTUM * momentum
+            )
 
     for fn in (
         start_rest,
@@ -759,6 +795,7 @@
         gain_z_sum,
         differ,
         add_x,
+        add_z,
         update,
     ):
         setattr(env, fn.__name__, fn)
@@ -779,25 +816,37 @@
             device_id_type=MESH,
         )
 
-    sent = []
-    for e in order:
+    sent, arrived = {}, []
+    for number, e in enumerate(order):
+        while arrived and arrived[0][0] < number - LAG:
+            sent.pop(arrived.pop(0)[1]).wait_send()
         for key, refs in e.needs:
             dst, target = refs()
             copy(key, dst, dst, target).wait_recv()
+            arrived.append((number, key))
         e.body()
         for key, _, _, refs in e.sends:
-            c = copy(key, *refs())
-            c.start()
-            sent.append(c)
-    for c in sent:
+            sent[key] = copy(key, *refs())
+            sent[key].start()
+    for c in sent.values():
         c.wait_send()
 
 
 def write_out(*refs):
     count = len(refs) // 2
     sem = refs[-1]
+    step = refs[0].shape[0] // PIECES
     copies = [
-        pltpu.make_async_copy(refs[i], refs[count + i], sem.at[i]) for i in range(count)
+        pltpu.make_async_copy(
+            refs[0].at[pl.ds(i * step, step)],
+            refs[count].at[pl.ds(i * step, step)],
+            sem.at[count + i],
+        )
+        for i in range(PIECES)
+    ]
+    copies += [
+        pltpu.make_async_copy(refs[i], refs[count + i], sem.at[i])
+        for i in range(1, count)
     ]
     for c in copies:
         c.start()
@@ -846,9 +895,11 @@
         vmem((fragments, length), f32),
         vmem((fragments, length), f32),
         vmem((fragments, length), f32),
-        vmem((RING, 1, length), f32),
         vmem((1, length), f32),
-        vmem((1, length), f32),
+        vmem((RING, 1, length // RING), f32),
+        vmem((1, length // RING), f32),
+        vmem((1, length // RING), f32),
+        vmem((RING, 1, length // RING), f32),
     ]
     for lo, hi, _ in SCATTER_PARTS:
         size = hi - lo
@@ -906,7 +957,7 @@
         out_shape=[jax.ShapeDtypeStruct(*s) for s in shapes],
         in_specs=[in_vmem] * len(shapes),
         out_specs=[in_hbm] * len(shapes),
-        scratch_shapes=[pltpu.SemaphoreType.DMA((len(shapes),))],
+        scratch_shapes=[pltpu.SemaphoreType.DMA((len(shapes) + PIECES,))],
         compiler_params=pltpu.CompilerParams(vmem_limit_bytes=2**20),
     )(*results)
     return (

time: 72.5 us -> 68.8 us (0.949)
  Pallas kernels: 70.4 us -> 66.4 us
    pallas_call x1, Pallas kernels: 68.3 us -> 64.3 us  [local(): pl.pallas_call(functools.partial(kernel, plan), out_shape=[vmem(*s) for s...]
where the time goes in v3:
time: 68.8 us; the launch traced here: 67.7 us
  Pallas kernels  66.4 us (97%)
  between operations  1.29 us (2%)
    pallas_call x1, Pallas kernels, local(): pl.pallas_call(functools.partial(kernel, plan), out_shape=[vmem(*s) for s...  64.3 us
    pallas_call x1, Pallas kernels, local(): pl.pallas_call(write_out, out_shape=[jax.ShapeDtypeStruct(*s) for s in sh...  2.1 us

profile of v3, /device:TPU:6, one launch (start us, length us, event | category | flops | bytes accessed | tf_op | source)
XLA Modules:
  0.0 67.7 jit_solution(2330640305046540748)
XLA Ops:
  1.3 64.3 %shard_map.119 = (bf16[256,7168]{1,0:T(8,128)(2,1)S(1)}, f32[224,512]{1,0:T(8,128)S(1)}, f32[1,224]{1,0:T(1,128)S(1)}, f32[1,16384]{1,0:T(1,128)S(1)}, f32[1,16384]{1,0:T(1,128)S(1)}) custom-call(bf16[256,7168]{1,0:T(8,128)(2,1)} %bitcast.8, f32[1,7168]{1,0:T(1,128)} %gain_all.1, bf16[224,512]{1,0:T(8,128)(2,1)} %bitcast.13, bf16[256,512]{1,0:T(8,128)(2,1)} %bitcast.12, ...), custom_call_target="tpu_custom_call" | custom-call | flops 3758096384 | bytes 16777216 | tf_op jit(solution)/shard_map/pallas_call | solution.py:932
  65.6 2.1 %shard_map.120 = (bf16[256,7168]{1,0:T(8,128)(2,1)}, f32[224,512]{1,0:T(8,128)}, f32[1,224]{1,0:T(1,128)}, f32[1,16384]{1,0:T(1,128)}, f32[1,16384]{1,0:T(1,128)}) custom-call(bf16[256,7168]{1,0:T(8,128)(2,1)S(1)} %get-tuple-element.15.refs_0_, f32[224,512]{1,0:T(8,128)S(1)} %get-tuple-element.16.refs_1_, f32[1,224]{1,0:T(1,128)S(1)} %get-tuple-element.17.refs_2_, ...), custom_call_target="tpu_custom_call" | custom-call | tf_op jit(solution)/shard_map/pallas_call | solution.py:955

commit v4 on v3

--- a/solution.py
+++ b/solution.py
@@ -15,16 +15,15 @@
 RING = 4
 NT = (((1,), (1,)), ((), ()))
 GATHER_PARTS = ((0, 224, "z"),)
-SCATTER_PARTS = ((0, 64, "y"), (64, 144, "y"), (144, 224, "z"))
+SCATTER_PARTS = ((0, 128, "y"), (128, 224, "z"))
 WIDTH = 512
 LAG = 12
 PIECES = 4
 ORDER = (
-    0, 16, 17, 18, 20, 22, 24, 19, 34, 54, 21, 78, 23, 94, 25, 58, 82, 38, 42, 26, 28, 4, 5, 35,
-    62, 98, 27, 29, 39, 36, 55, 95, 56, 2, 1, 30, 31, 57, 84, 79, 74, 3, 32, 70, 40, 11, 96, 37,
-    10, 86, 50, 6, 7, 83, 75, 8, 76, 99, 14, 97, 64, 33, 87, 13, 88, 63, 43, 101, 102, 41, 80,
-    51, 12, 85, 60, 59, 103, 46, 44, 66, 9, 15, 65, 72, 105, 77, 90, 100, 61, 71, 106, 104, 48,
-    47, 45, 52, 67, 68, 81, 92, 89, 91, 107, 49, 109, 69, 73, 53, 108, 93,
+    0, 16, 17, 18, 20, 22, 24, 19, 34, 21, 58, 78, 23, 25, 42, 74, 38, 54, 4, 5, 26, 27, 36, 35,
+    75, 1, 2, 28, 66, 29, 62, 55, 3, 60, 37, 30, 32, 59, 8, 7, 56, 50, 31, 76, 63, 64, 33, 10,
+    11, 79, 14, 13, 39, 40, 6, 67, 43, 81, 44, 9, 83, 12, 46, 68, 57, 70, 15, 82, 85, 41, 84,
+    51, 86, 45, 52, 47, 48, 77, 65, 61, 71, 80, 72, 87, 89, 49, 69, 73, 53, 88,
 )
 OPPOSITE = {1: 3, 3: 1, 2: 2}
 CHUNKS = ((2, 1), (1, 1), (3, 1), (2, 0), (0, 1), (1, 0), (3, 0), (0, 0))

time: 68.8 us -> 68.1 us (0.990)
  no operation moved by 1% of the time
where the time goes in v4:
time: 68.1 us; the launch traced here: 67.7 us
  Pallas kernels  66.4 us (98%)
  between operations  1.29 us (2%)
    pallas_call x1, Pallas kernels, local(): pl.pallas_call(functools.partial(kernel, plan), out_shape=[vmem(*s) for s...  64.3 us
    pallas_call x1, Pallas kernels, local(): pl.pallas_call(write_out, out_shape=[jax.ShapeDtypeStruct(*s) for s in sh...  2.1 us

profile of v4, /device:TPU:6, one launch (start us, length us, event | category | flops | bytes accessed | tf_op | source)
XLA Modules:
  0.0 67.7 jit_solution(13059634601038909914)
XLA Ops:
  1.3 64.3 %shard_map.119 = (bf16[256,7168]{1,0:T(8,128)(2,1)S(1)}, f32[224,512]{1,0:T(8,128)S(1)}, f32[1,224]{1,0:T(1,128)S(1)}, f32[1,16384]{1,0:T(1,128)S(1)}, f32[1,16384]{1,0:T(1,128)S(1)}) custom-call(bf16[256,7168]{1,0:T(8,128)(2,1)} %bitcast.8, f32[1,7168]{1,0:T(1,128)} %gain_all.1, bf16[224,512]{1,0:T(8,128)(2,1)} %bitcast.13, bf16[256,512]{1,0:T(8,128)(2,1)} %bitcast.12, ...), custom_call_target="tpu_custom_call" | custom-call | flops 3758096384 | bytes 16777216 | tf_op jit(solution)/shard_map/pallas_call | solution.py:931
  65.6 2.1 %shard_map.120 = (bf16[256,7168]{1,0:T(8,128)(2,1)}, f32[224,512]{1,0:T(8,128)}, f32[1,224]{1,0:T(1,128)}, f32[1,16384]{1,0:T(1,128)}, f32[1,16384]{1,0:T(1,128)}) custom-call(bf16[256,7168]{1,0:T(8,128)(2,1)S(1)} %get-tuple-element.15.refs_0_, f32[224,512]{1,0:T(8,128)S(1)} %get-tuple-element.16.refs_1_, f32[1,224]{1,0:T(1,128)S(1)} %get-tuple-element.17.refs_2_, ...), custom_call_target="tpu_custom_call" | custom-call | tf_op jit(solution)/shard_map/pallas_call | solution.py:954
